TPU v7x, 128 devices: a whole 4x4x4 slice. The times are simulated.
128 devices in a mesh: row: 8 (over x, core), col: 16 (over y, z).
Axes of the slice: x: 4, y: 4, z: 4, core: 2. Of those that a mesh axis runs over, the one named last changes fastest.
Arguments:
- atom_feat: bfloat16 [16384, 128], P(('row', 'col')), may hold values from -6 to 6
- atom_token: int32 [16384], P(('row', 'col')), may hold values from 0 to 2047, as said below
- w_atom_qkv: bfloat16 [128, 384], replicated, may hold values from -0.5 to 0.5
- w_atom_out: bfloat16 [128, 128], replicated, may hold values from -0.5 to 0.5
- w_atom_up: bfloat16 [128, 768], replicated, may hold values from -0.5 to 0.5
- pair_repr: bfloat16 [2048, 8, 256, 128], P('row', None, 'col'), may hold values from -6 to 6
- w_bias: float32 [128, 16], replicated, may hold values from -16 to 16
- w_query: bfloat16 [768, 768], replicated, may hold values from -0.21875 to 0.21875
- w_kv: bfloat16 [768, 1536], replicated, may hold values from -0.21875 to 0.21875
- w_gate: bfloat16 [768, 768], replicated, may hold values from -0.21875 to 0.21875
- w_out: bfloat16 [768, 768], replicated, may hold values from -0.21875 to 0.21875
- w_down: bfloat16 [768, 128], replicated, may hold values from -0.21875 to 0.21875
Outputs:
- token_out: bfloat16 [2048, 768], P('row', 'col')
- atom_final: bfloat16 [16384, 128], P(('row', 'col'))
Inputs may be any that keep to these rules, and one draw needn't show every extreme that they name: atom_token never falls along the atoms; the atoms held by the device with index r along row name only tokens r*256 to r*256 + 255, and every token is named by at least one atom.
All inputs are finite; a program needn't handle non-finite values.
Results may differ from a plain program's by a relative error of at most 0.017.
The roundings to bfloat16 on the way count: a program that leaves them out, or rounds other values in their place, can miss the bound.
Values may be sent and summed in bfloat16 or wider, within the bound.
A program may use at most 192 MiB of HBM per device.

v0:
```python
import jax
import jax.numpy as jnp
from jax import lax
from jax.sharding import PartitionSpec as P

AHEADS = 4
QBLOCK = 32
KWIN = 128
HALO = 48


EPS = 1e-05


def with_halo(cells, sides, width):
    for axis, dim in sides:
        count = lax.axis_size(axis)
        ends = count - 1
        head = lax.slice_in_dim(cells, 0, width, axis=dim)
        tail = lax.slice_in_dim(cells, cells.shape[dim] - width, cells.shape[dim], axis=dim)
        cells = jnp.concatenate(
            [
                lax.ppermute(tail, axis, [(i, (i + 1) % count) for i in range(ends)]),
                cells,
                lax.ppermute(head, axis, [((i + 1) % count, i) for i in range(ends)]),
            ],
            axis=dim,
        )
    return cells


def layer_norm(values):
    center = jnp.mean(values, axis=-1, keepdims=True)
    spread = jnp.mean(values * values, axis=-1, keepdims=True) - center * center
    return (values - center) / jnp.sqrt(spread + EPS)


def atom_layer(atom_feat, w_atom_qkv, w_atom_out, flat_index, all_atoms):
    atom_count, channels = atom_feat.shape
    head_size = channels // AHEADS
    atom_proj = jnp.dot(atom_feat, w_atom_qkv, preferred_element_type=jnp.float32).astype(
        jnp.bfloat16
    )
    queries = atom_proj[:, :channels]
    keyvals = with_halo(atom_proj[:, channels:], ((("row", "col"), 0),), HALO)
    blocks = atom_count // QBLOCK
    window = jnp.arange(blocks)[:, None] * QBLOCK + jnp.arange(KWIN)[None, :]
    position = flat_index * atom_count + window - HALO
    valid = (position >= 0) & (position < all_atoms)
    near = keyvals[window]
    near_keys = near[..., :channels].reshape(blocks, KWIN, AHEADS, head_size)
    near_vals = near[..., channels:].reshape(blocks, KWIN, AHEADS, head_size)
    block_q = queries.reshape(blocks, QBLOCK, AHEADS, head_size)
    scores = (
        jnp.einsum("bqhd,bkhd->bhqk", block_q, near_keys, preferred_element_type=jnp.float32)
        / head_size**0.5
    )
    scores = jnp.where(valid[:, None, None, :], scores, -1e30)
    top = jnp.max(scores, axis=-1, keepdims=True)
    expo = jnp.exp(scores - top)
    atom_weights = expo.astype(jnp.bfloat16)
    denom = jnp.sum(expo, axis=-1)
    context = jnp.einsum(
        "bhqk,bkhd->bqhd", atom_weights, near_vals, preferred_element_type=jnp.float32
    )
    context = context / jnp.transpose(denom, (0, 2, 1))[..., None]
    atom_ctx = context.reshape(atom_count, channels).astype(jnp.bfloat16)
    mixed = atom_feat.astype(jnp.float32) + jnp.dot(
        atom_ctx, w_atom_out, preferred_element_type=jnp.float32
    )
    return mixed.astype(jnp.bfloat16)


def body(
    atom_feat,
    atom_token,
    w_atom_qkv,
    w_atom_out,
    w_atom_up,
    pair_repr,
    w_bias,
    w_query,
    w_kv,
    w_gate,
    w_out,
    w_down,
):
    row_count = lax.axis_size("row")
    col_count = lax.axis_size("col")
    row_index = lax.axis_index("row")
    col_index = lax.axis_index("col")
    atom_count = atom_feat.shape[0]
    tok_rows = pair_repr.shape[0]
    key_share = pair_repr.shape[2]
    pair_width = pair_repr.shape[3]
    head_count = w_bias.shape[1]
    model_width = w_query.shape[0]
    head_size = model_width // head_count
    chan_share = model_width // col_count
    flat_index = row_index * col_count + col_index
    atom_out = atom_layer(
        atom_feat, w_atom_qkv, w_atom_out, flat_index, atom_count * row_count * col_count
    )
    atom_up = jax.nn.relu(jnp.dot(atom_out, w_atom_up, preferred_element_type=jnp.float32)).astype(
        jnp.bfloat16
    )
    local_token = atom_token - row_index * tok_rows
    one_hot = (local_token[:, None] == jnp.arange(tok_rows, dtype=jnp.int32)[None, :]).astype(
        jnp.bfloat16
    )
    partial_sum = lax.dot_general(
        one_hot, atom_up, (((0,), (0,)), ((), ())), preferred_element_type=jnp.float32
    )
    count_part = jnp.sum(one_hot.astype(jnp.float32), axis=0)
    chan_start = col_index * chan_share
    totals, counts = (
        lax.psum(partial_sum.astype(jnp.bfloat16), "col").astype(jnp.float32),
        lax.psum(count_part.astype(jnp.bfloat16), "col").astype(jnp.float32),
    )
    token_act = totals / counts[:, None]
    normed = layer_norm(token_act).astype(jnp.bfloat16)
    act_share = lax.dynamic_slice_in_dim(token_act, chan_start, chan_share, 1)
    queries = jnp.dot(normed, w_query, preferred_element_type=jnp.float32).astype(jnp.bfloat16)
    gating = jax.nn.sigmoid(jnp.dot(normed, w_gate, preferred_element_type=jnp.float32))
    key_source = lax.dynamic_slice_in_dim(normed, col_index * key_share, key_share, 0)
    keyvals_local = jnp.dot(key_source, w_kv, preferred_element_type=jnp.float32).astype(
        jnp.bfloat16
    )
    keyvals_rows = lax.all_gather(keyvals_local, "row", axis=0, tiled=True)
    pair_normed = layer_norm(pair_repr.astype(jnp.float32)).astype(jnp.bfloat16)
    pair_bias = jnp.dot(
        pair_normed.reshape(-1, pair_width),
        w_bias.astype(jnp.bfloat16),
        preferred_element_type=jnp.float32,
    ).astype(jnp.bfloat16)
    pair_bias = jnp.transpose(
        pair_bias.reshape(tok_rows, row_count * key_share, head_count), (2, 0, 1)
    )
    query_heads = queries.reshape(tok_rows, head_count, head_size)
    keyvals_all = lax.all_gather(keyvals_rows, "col", axis=0, tiled=True)
    bias_all = lax.all_gather(pair_bias, "col", axis=2, tiled=True)
    key_count = keyvals_all.shape[0]
    key_heads = keyvals_all[:, :model_width].reshape(key_count, head_count, head_size)
    val_heads = keyvals_all[:, model_width:].reshape(key_count, head_count, head_size)
    scores = (
        jnp.einsum("qhd,khd->hqk", query_heads, key_heads, preferred_element_type=jnp.float32)
        / head_size**0.5
    )
    scores = scores + bias_all.astype(jnp.float32)
    top = jnp.max(scores, axis=-1, keepdims=True)
    expo = jnp.exp(scores - top)
    token_weights = expo.astype(jnp.bfloat16)
    denom = jnp.sum(expo, axis=-1)
    weighted = jnp.einsum(
        "hqk,khd->qhd", token_weights, val_heads, preferred_element_type=jnp.float32
    )
    context = weighted / jnp.transpose(denom)[:, :, None]
    gated = (context.reshape(tok_rows, model_width) * gating).astype(jnp.bfloat16)
    out_cols = lax.dynamic_slice_in_dim(w_out, chan_start, chan_share, 1)
    token_share = (act_share + jnp.dot(gated, out_cols, preferred_element_type=jnp.float32)).astype(
        jnp.bfloat16
    )
    down_rows = lax.dynamic_slice_in_dim(w_down, chan_start, chan_share, 0)
    down_part = jnp.dot(token_share, down_rows, preferred_element_type=jnp.float32)
    token_down = lax.psum(down_part.astype(jnp.bfloat16), "col")
    atom_final = atom_out.astype(jnp.float32) + jnp.dot(
        one_hot, token_down, preferred_element_type=jnp.float32
    )
    return (token_share, atom_final.astype(jnp.bfloat16))


def solution(mesh):
    return jax.shard_map(
        body,
        mesh=mesh,
        in_specs=(
            P(("row", "col"), None),
            P(("row", "col")),
            P(),
            P(),
            P(),
            P("row", None, "col", None),
            P(),
            P(),
            P(),
            P(),
            P(),
            P(),
        ),
        out_specs=(P("row", "col"), P(("row", "col"), None)),
        check_vma=False,
    )
```

profile of v0, /device:TPU:1, one launch (start us, length us, event | category | flops | bytes accessed | tf_op | source)
XLA Modules:
  0.0 453.5 jit_solution(2126904816005425749)
XLA Ops:
  8.5 4.4 collective-permute-start
  12.9 7.1 %collective-permute-start.1 = (bf16[48,256]{1,0:T(8,128)(2,1)S(1)}, bf16[48,256]{1,0:T(8,128)(2,1)S(1)}, u32[]{:S(2)}, u32[]{:S(2)}) collective-permute-start(bf16[48,256]{1,0:T(8,128)(2,1)S(1)} %get-tuple-element.25), channel_id=1, source_target_pairs={{1,0},{2,1},{3,2},{4,3},{5,4},{6,5},{7,6},{8,7},{9,8},{10,9},{11,1... | collective-permute-start | bytes 73736 | tf_op jit(solution)/shard_map/ppermute | solution.py:25
  20.9 2.0 gather_fusion
  25.3 2.1 convolution_convert_fusion.3
  27.6 34.5 %psum.22 = bf16[256]{0:T(256)(128)(2,1)S(1)} all-reduce(bf16[256]{0:T(256)(128)(2,1)S(1)} %fusion.38), channel_id=1, replica_groups=mesh['row'=8,'col'=16] {'col'}, use_global_device_ids=true, to_apply=%region_4.5 | all-reduce | flops 256 | bytes 1024 | tf_op jit(solution)/shard_map/psum | solution.py:118
  62.0 50.0 %all-reduce.3.cloned.1.call-done = bf16[256,768]{1,0:T(8,128)(2,1)} async-done(((bf16[256,768]{1,0:T(8,128)(2,1)}), bf16[256,768]{1,0:T(8,128)(2,1)}) %all-reduce.3.cloned.1.call-update) | async-done | bytes 393232 | tf_op jit(solution)/shard_map/psum | solution.py:117
  112.0 1.3 fusion.53
  113.3 2.1 convert_divide_fusion
  115.9 16.2 %all_gather.9 = bf16[128,1536]{1,0:T(8,128)(2,1)} all-gather(bf16[16,1536]{1,0:T(8,128)(2,1)S(1)} %convolution_convert_fusion.1), channel_id=1, replica_groups=mesh['row'=8,'col'=16] {'row'}, dimensions={0}, use_global_device_ids=true | all-gather | bytes 442368 | tf_op jit(solution)/shard_map/all_gather | solution.py:129
  132.2 10.7 %convert_reduce_fusion = (f32[256,8,16]{2,1,0:T(8,128)S(1)}, f32[256,8,16]{2,1,0:T(8,128)S(1)}) fusion(bf16[256,8,16,128]{3,2,1,0:T(8,128)(2,1)} %param.17), kind=kLoop, calls=%fused_computation.8 | loop fusion | flops 16711680 | bytes 8650752 | tf_op jit(solution)/shard_map/reduce_sum | solution.py:33
  144.5 11.1 %fusion.3 = bf16[256,8,16,128]{3,2,1,0:T(8,128)(2,1)S(1)} fusion(bf16[256,8,16,128]{3,2,1,0:T(8,128)(2,1)} %param.17, f32[256,8,16]{2,1,0:T(8,128)S(1)} %copy.63, f32[256,8,16]{2,1,0:T(8,128)S(1)} %copy.61), kind=kLoop, calls=%fused_computation.10 | loop fusion | flops 16777216 | bytes 17039360 | tf_op jit(solution)/shard_map/convert_element_type | solution.py:130
  155.6 2.3 fusion.8
  160.1 31.7 %all-gather.3.cloned.1.call-done = bf16[2048,1536]{1,0:T(8,128)(2,1)} async-done(((bf16[128,1536]{1,0:T(8,128)(2,1)}), bf16[2048,1536]{1,0:T(8,128)(2,1)}) %all-gather.3.cloned.1.call-update) | async-done | bytes 6291472 | tf_op jit(solution)/shard_map/all_gather | solution.py:140
  191.8 5.9 %fusion.54 = (bf16[2048,768]{1,0:T(8,128)(2,1)}, bf16[2048,768]{1,0:T(8,128)(2,1)}) fusion(bf16[2048,1536]{1,0:T(8,128)(2,1)} %all-gather.3.cloned.1.call-done), kind=kLoop, calls=%fused_computation.81 | loop fusion | bytes 12582912 | tf_op jit(solution)/shard_map/slice | solution.py:143
  197.7 4.7 %copy.59 = bf16[2048,768]{0,1:T(8,128)(2,1)} copy(bf16[2048,768]{1,0:T(8,128)(2,1)} %get-tuple-element.16) | data formatting | bytes 6291456 | tf_op jit(solution)/shard_map/slice | solution.py:143
  202.5 4.8 %copy.57 = bf16[2048,768]{0,1:T(8,128)(2,1)} copy(bf16[2048,768]{1,0:T(8,128)(2,1)} %get-tuple-element.17) | data formatting | bytes 6291456 | tf_op jit(solution)/shard_map/slice | solution.py:144
  207.3 106.6 %all-gather.5.cloned.1.call-done = bf16[16,256,2048]{2,1,0:T(8,128)(2,1)} async-done(((bf16[16,256,128]{2,1,0:T(8,128)(2,1)}), bf16[16,256,2048]{2,1,0:T(8,128)(2,1)}) %all-gather.5.cloned.1.call-update) | async-done | bytes 16777232 | tf_op jit(solution)/shard_map/all_gather | solution.py:141
  313.9 17.7 %fusion.58 = (f32[16,256]{1,0:T(8,128)S(1)}, f32[16,256,2048]{2,1,0:T(8,128)}) fusion(bf16[16,256,2048]{2,1,0:T(8,128)(2,1)} %all-gather.5.cloned.1.call-done, bf16[256,16,48]{0,2,1:T(8,128)(2,1)S(1)} %bitcast.53, bf16[2048,16,48]{0,2,1:T(8,128)(2,1)} %bitcast.49), kind=kOutput, calls=%fused_computation.85 | convolution fusion | flops 838856704 | bytes 53886976 | tf_op jit(solution)/shard_map/qhd,khd->hqk/dot_general | solution.py:146
  331.6 14.2 %fusion = f32[16,256]{1,0:T(8,128)} fusion(f32[16,256,2048]{2,1,0:T(8,128)} %get-tuple-element.31, f32[16,256]{1,0:T(8,128)S(1)} %get-tuple-element.30), kind=kLoop, calls=%fused_computation.4 | loop fusion | flops 16773120 | bytes 33587200 | tf_op jit(solution)/shard_map/reduce_sum | solution.py:153
  345.8 14.8 %fusion.22 = f32[256,16,48]{0,2,1:T(8,128)S(1)} fusion(bf16[2048,16,48]{0,2,1:T(8,128)(2,1)} %bitcast.50, f32[16,256,2048]{2,1,0:T(8,128)} %get-tuple-element.31, f32[16,256]{1,0:T(8,128)S(1)} %get-tuple-element.30, f32[256,16]{0,1:T(8,128)} %bitcast.57), kind=kOutput, calls=%fused_computation.33 | convolution fusion | flops 822280192 | bytes 37519360 | tf_op jit(solution)/shard_map/hqk,khd->qhd/dot_general | solution.py:154
  361.8 2.4 fusion.26
  364.1 1.5 convolution_convert_fusion.5
  366.3 79.0 %all-reduce.5.cloned.1.call-done = bf16[256,128]{1,0:T(8,128)(2,1)} async-done(((bf16[256,128]{1,0:T(8,128)(2,1)}), bf16[256,128]{1,0:T(8,128)(2,1)}) %all-reduce.5.cloned.1.call-update) | async-done | bytes 65552 | tf_op jit(solution)/shard_map/psum | solution.py:165
  445.3 1.7 fusion.28
  (56 shorter events, 10.9 us)
Async XLA Ops:
  7.2 108.3 %copy-start = (bf16[768,1536]{1,0:T(8,128)(2,1)S(1)}, bf16[768,1536]{1,0:T(8,128)(2,1)}, u32[]{:S(2)}) copy-start(bf16[768,1536]{1,0:T(8,128)(2,1)} %param.20) | copy-start | bytes 7077892
  7.2 104.9 %all-reduce.3.cloned.1.call-start = ((), (), s32[]{:S(2)}) async-start(), calls=%async_computation | async-start | bytes 786432 | tf_op jit(solution)/shard_map/psum | solution.py:117
  8.5 12.4 %collective-permute-start = (bf16[48,256]{1,0:T(8,128)(2,1)S(1)}, bf16[48,256]{1,0:T(8,128)(2,1)S(1)}, u32[]{:S(2)}, u32[]{:S(2)}) collective-permute-start(bf16[48,256]{1,0:T(8,128)(2,1)S(1)} %get-tuple-element.24), channel_id=1, source_target_pairs={{0,1},{1,2},{2,3},{3,4},{4,5},{5,6},{6,7},{7,8},{8,9},{9,10},{10,1... | collective-permute-start | bytes 73736 | tf_op jit(solution)/shard_map/ppermute | solution.py:23
  12.9 8.1 %collective-permute-start.1 = (bf16[48,256]{1,0:T(8,128)(2,1)S(1)}, bf16[48,256]{1,0:T(8,128)(2,1)S(1)}, u32[]{:S(2)}, u32[]{:S(2)}) collective-permute-start(bf16[48,256]{1,0:T(8,128)(2,1)S(1)} %get-tuple-element.25), channel_id=1, source_target_pairs={{1,0},{2,1},{3,2},{4,3},{5,4},{6,5},{7,6},{8,7},{9,8},{10,9},{11,1... | collective-permute-start | bytes 73736 | tf_op jit(solution)/shard_map/ppermute | solution.py:25
  20.7 122.1 %copy-start.5 = (s32[128]{0:T(128)}, s32[128]{0:T(128)S(1)}, u32[]{:S(2)}) copy-start(s32[128]{0:T(128)S(1)} %broadcast_subtract_fusion) | copy-start | bytes 1540
  25.3 117.6 %copy-start.3 = (bf16[128,128]{1,0:T(8,128)(2,1)}, bf16[128,128]{1,0:T(8,128)(2,1)S(1)}, u32[]{:S(2)}) copy-start(bf16[128,128]{1,0:T(8,128)(2,1)S(1)} %fusion.27) | copy-start | bytes 98308
  27.4 164.4 %all-gather.3.cloned.1.call-start = ((), (), s32[]{:S(2)}) async-start(), calls=%async_computation.1 | async-start | bytes 6684672 | tf_op jit(solution)/shard_map/all_gather | solution.py:140
  132.1 181.8 %all-gather.5.cloned.1.call-start = ((), (), s32[]{:S(2)}) async-start(), calls=%async_computation.2 | async-start | bytes 17825792 | tf_op jit(solution)/shard_map/all_gather | solution.py:141
  144.5 11.1 %copy-start.4 = (f32[128,16]{0,1:T(8,128)S(1)}, f32[128,16]{0,1:T(8,128)}, u32[]{:S(2)}) copy-start(f32[128,16]{0,1:T(8,128)} %param.18) | copy-start | bytes 24580
  155.6 3.8 copy-start.2
  159.2 286.1 %all-reduce.5.cloned.1.call-start = ((), (), s32[]{:S(2)}) async-start(), calls=%async_computation.3 | async-start | bytes 131072 | tf_op jit(solution)/shard_map/psum | solution.py:165
  345.8 101.2 %copy-start.1 = (bf16[768,1536]{1,0:T(8,128)(2,1)S(1)}, bf16[768,1536]{1,0:T(8,128)(2,1)}, u32[]{:S(2)}) copy-start(bf16[768,1536]{1,0:T(8,128)(2,1)} %param.20) | copy-start | bytes 7077892
Sparse Core Ops, SparseCore 0:
  27.6 84.4 all-reduce.2
  132.2 59.5 all-gather.2
  193.9 119.8 all-gather.4
  365.8 79.5 all-reduce.4
where the time goes:
time: 455 us; the launch traced here: 454 us
  waiting for transfers between devices  267 us (59%)
  blocking collectives  50.7 us (11%)
  matrix products  46 us (10%)
  other arithmetic  40.6 us (9%)
  local copies, waits for them, and re-layouts  23 us (5%)
  between operations  14.1 us (3%)
  starting transfers between devices  11.8 us (3%)
    all_gather x1, waiting for transfers between devices, body(): bias_all = lax.all_gather(pair_bias, 'col', axis=2, tiled=True)  107 us
    psum x1, waiting for transfers between devices, body(): token_down = lax.psum(down_part.astype(jnp.bfloat16), 'col')  79 us
    psum x1, waiting for transfers between devices, body(): lax.psum(partial_sum.astype(jnp.bfloat16), 'col').astype(jnp.float32)  50 us
    psum x1, blocking collectives, body(): lax.psum(count_part.astype(jnp.bfloat16), 'col').astype(jnp.float32)  34.5 us
    all_gather x1, waiting for transfers between devices, body(): keyvals_all = lax.all_gather(keyvals_rows, 'col', axis=0, tiled=True)  31.7 us
    dot_general x1, matrix products, body(): jnp.einsum('qhd,khd->hqk', query_heads, key_heads, preferred_element_type...  17.7 us
    all_gather x1, blocking collectives, body(): keyvals_rows = lax.all_gather(keyvals_local, 'row', axis=0, tiled=True)  16.2 us
    dot_general x1, matrix products, body(): jnp.einsum('hqk,khd->qhd', token_weights, val_heads, preferred_element_ty...  14.8 us
  transfers between devices with their start and end apart: 6, of which 4 were waited for; matrix products, arithmetic and copies ran while one was open for 10% of the time, Pallas kernels for 0%

commit v1 on v0

v1 whole, which is shorter than its diff:
```python
import functools

import jax
import jax.numpy as jnp
from jax import lax
from jax.experimental import pallas as pl
from jax.experimental.pallas import tpu as pltpu
from jax.sharding import PartitionSpec as P

MESH = pl.DeviceIdType.MESH
F32 = jnp.float32
BF16 = jnp.bfloat16

EPS = 1e-05
AHEADS = 4
QBLOCK = 32
KWIN = 128
HALO = 48
EXT = 256
CHUNK = 16
PIECES = 4
LANES = 128
VOFF = 64
WINDOW = 256


def dot(a, b, dims=((1,), (0,))):
    return lax.dot_general(a, b, (dims, ((), ())), preferred_element_type=F32)


def iota(shape, dim):
    return lax.broadcasted_iota(jnp.int32, shape, dim)


def kernel(
    feat, tok, w_qkv, w_ao, w_up, pair, w_bias, w_query, w_kv, w_gate, w_out, w_down,
    out_tok, out_atom,
    xbuf, v_qkv, v_ao, v_up, v_bias, v_q, v_k, v_v, v_g, v_o, v_d,
    ext, tok_all, atoms_all, onehot, stage, bias_out, bias_in,
    wsel, w_out_t, act_t, kv_own, kv_all, g_all,
    load_sem, pair_sem, halo_send, halo_recv, tok_send, tok_recv,
    atom_send, atom_recv, bias_send, bias_recv, kv_send, kv_recv, g_send, g_recv,
):
    rows, cols = lax.axis_size("row"), lax.axis_size("col")
    r, c = lax.axis_index("row"), lax.axis_index("col")
    flat = r * cols + c
    devices = rows * cols
    atoms, chans = feat.shape
    tokens, _, share, _ = pair.shape
    keys = rows * share
    width = w_query.shape[0]
    head = width // cols

    loads = []

    def load(src, dst, sem=None):
        copy = pltpu.make_async_copy(src, dst, load_sem.at[len(loads)] if sem is None else sem)
        copy.start()
        if sem is None:
            loads.append(copy)
        return copy

    load_feat = load(feat, ext.at[pl.ds(HALO, atoms)])
    load_tok = load(tok, tok_all.at[c])
    load_bias = load(w_bias, v_bias)
    part = tokens // PIECES
    load_pair = [load(pair.at[pl.ds(0, part)], xbuf.at[pl.ds(0, part)], pair_sem.at[0])]
    load_qkv = load(w_qkv, v_qkv)
    load_ao = load(w_ao, v_ao)
    for i in range(1, PIECES):
        load_pair.append(
            load(pair.at[pl.ds(i * part, part)], xbuf.at[pl.ds(i * part, part)], pair_sem.at[i])
        )
    load_up = load(w_up, v_up)
    first = jnp.minimum(c * head // LANES, (width - WINDOW) // LANES)
    begin = pl.multiple_of(first * LANES, LANES)
    window = pl.ds(begin, WINDOW)
    load_q = load(w_query.at[:, window], v_q)
    load_g = load(w_gate.at[:, window], v_g)
    load_k = load(w_kv.at[:, window], v_k)
    load_v = load(w_kv.at[:, pl.ds(pl.multiple_of(width + begin, LANES), WINDOW)], v_v)
    load_o = load(w_out, v_o)
    load_d = load(w_down, v_d)

    barrier = pltpu.get_barrier_semaphore()
    right, left = lax.rem(flat + 1, devices), lax.rem(flat + devices - 1, devices)

    def coords(index):
        return (index // cols, lax.rem(index, cols))

    for peer in (left, right):
        pl.semaphore_signal(barrier, inc=1, device_id=coords(peer), device_id_type=MESH)
    for d in range(1, cols):
        pl.semaphore_signal(
            barrier, inc=1, device_id=(r, lax.rem(c + d, cols)), device_id_type=MESH
        )
    for d in range(1, rows):
        pl.semaphore_signal(
            barrier, inc=1, device_id=(lax.rem(r + d, rows), c), device_id_type=MESH
        )
    ext[pl.ds(atoms + 2 * HALO, EXT - atoms - 2 * HALO), :] = jnp.zeros(
        (EXT - atoms - 2 * HALO, chans), BF16
    )
    pl.semaphore_wait(barrier, cols + rows)

    to_right = pltpu.make_async_remote_copy(
        src_ref=feat.at[pl.ds(atoms - HALO, HALO)],
        dst_ref=ext.at[pl.ds(0, HALO)],
        send_sem=halo_send.at[0],
        recv_sem=halo_recv.at[0],
        device_id=coords(right),
        device_id_type=MESH,
    )
    to_left = pltpu.make_async_remote_copy(
        src_ref=feat.at[pl.ds(0, HALO)],
        dst_ref=ext.at[pl.ds(HALO + atoms, HALO)],
        send_sem=halo_send.at[1],
        recv_sem=halo_recv.at[1],
        device_id=coords(left),
        device_id_type=MESH,
    )
    to_right.start()
    to_left.start()

    def col_copy(src, dst, send, recv, d):
        return pltpu.make_async_remote_copy(
            src_ref=src,
            dst_ref=dst,
            send_sem=send.at[d],
            recv_sem=recv.at[d],
            device_id=(r, lax.rem(c + d, cols)),
            device_id_type=MESH,
        )

    load_tok.wait()
    tok_copies = [
        col_copy(tok_all.at[c], tok_all.at[c], tok_send, tok_recv, d) for d in range(1, cols)
    ]
    for copy in tok_copies:
        copy.start()

    load_bias.wait()
    eye = (iota((LANES, LANES), 0) == iota((LANES, LANES), 1)).astype(BF16)
    wb_t = dot(v_bias[...].astype(BF16), eye, ((0,), (0,))).astype(BF16)
    wb_sum = jnp.sum(wb_t.astype(F32), axis=1, keepdims=True)
    heads = wb_t.shape[0]
    lhs = jnp.concatenate([wb_t, jnp.ones((16, LANES), BF16)], axis=0)
    ones = jnp.ones((16, LANES), BF16)

    def pair_chunk(index):
        start = pl.multiple_of(index * CHUNK, CHUNK)
        x = xbuf[pl.ds(start, CHUNK)].reshape(CHUNK * keys, LANES)
        x32 = x.astype(F32)
        square = x32 * x32
        high = square.astype(BF16)
        low = (square - high.astype(F32)).astype(BF16)
        proj = dot(lhs, x, ((1,), (1,)))
        squares = dot(ones, high, ((1,), (1,))) + dot(ones, low, ((1,), (1,)))
        mean = proj[heads:heads + 8] * (1.0 / LANES)
        var = squares[:8] * (1.0 / LANES) - mean * mean
        scale = lax.rsqrt(var + EPS)
        mean = jnp.concatenate([mean] * (heads // 8), axis=0)
        scale = jnp.concatenate([scale] * (heads // 8), axis=0)
        bias = (proj[:heads] - mean * wb_sum) * scale
        for q in range(CHUNK):
            stage[pl.ds(q, heads, stride=CHUNK), :] = bias[:, q * keys:(q + 1) * keys]
        for h in range(heads):
            bias_out[h, pl.ds(start, CHUNK), :] = stage[pl.ds(h * CHUNK, CHUNK), :].astype(BF16)

    def bias_copy(i, d):
        span = pl.ds(i * part, part)
        return col_copy(
            bias_out.at[lax.rem(c + d, cols), span], bias_in.at[c, span], bias_send, bias_recv, d
        )

    def pair_piece(i):
        load_pair[i].wait()
        steps = part // CHUNK

        def step(k, carry):
            pair_chunk(i * steps + k)
            return carry

        lax.fori_loop(0, steps, step, 0)

    def send_piece(i):
        for d in range(1, cols):
            bias_copy(i, d).start()

    pair_piece(0)

    load_feat.wait()
    load_qkv.wait()
    load_ao.wait()
    to_right.wait()
    to_left.wait()
    proj = dot(ext[...], v_qkv[...]).astype(BF16)
    queries = proj[HALO:HALO + atoms, :chans]
    near_keys = proj[:, chans:2 * chans]
    near_vals = proj[:, 2 * chans:]
    lane_head = iota((atoms, chans), 1) // (chans // AHEADS)
    by_head = jnp.concatenate(
        [jnp.where(lane_head == h, queries, jnp.zeros_like(queries)) for h in range(AHEADS)], axis=0
    )
    scores = dot(by_head, near_keys, ((1,), (1,))) * (chans // AHEADS) ** -0.5
    block = lax.rem(iota(scores.shape, 0), atoms) // QBLOCK * QBLOCK
    offset = iota(scores.shape, 1)
    position = flat * atoms + offset - HALO
    valid = (offset >= block) & (offset < block + KWIN)
    valid = valid & (position >= 0) & (position < devices * atoms)
    scores = jnp.where(valid, scores, -1e30)
    expo = jnp.exp(scores - jnp.max(scores, axis=1, keepdims=True))
    denom = jnp.sum(expo, axis=1, keepdims=True)
    mixed = dot(expo.astype(BF16), near_vals) / denom
    context = jnp.zeros((atoms, chans), F32)
    for h in range(AHEADS):
        context = jnp.where(lane_head == h, mixed[h * atoms:(h + 1) * atoms], context)
    atom_out = ext[pl.ds(HALO, atoms), :].astype(F32) + dot(context.astype(BF16), v_ao[...])
    atoms_all[c] = atom_out.astype(BF16)
    atom_copies = [
        col_copy(atoms_all.at[c], atoms_all.at[c], atom_send, atom_recv, d) for d in range(1, cols)
    ]
    for copy in atom_copies:
        copy.start()

    send_piece(0)
    for i in range(1, PIECES):
        pair_piece(i)
        send_piece(i)

    load_q.wait()
    load_g.wait()
    load_k.wait()
    load_v.wait()
    source = iota((WINDOW, LANES), 0) - (c * head - begin)
    target = iota((WINDOW, LANES), 1)
    pick_low = ((source == target) & (target < head)).astype(BF16)
    pick_high = ((source == target - VOFF) & (target >= VOFF) & (target < VOFF + head)).astype(BF16)
    wsel[:, 0:LANES] = dot(v_q[...], pick_low).astype(BF16)
    wsel[:, LANES:2 * LANES] = dot(v_g[...], pick_high).astype(BF16)
    wsel[:, 2 * LANES:] = (dot(v_k[...], pick_low) + dot(v_v[...], pick_high)).astype(BF16)

    for copy in tok_copies:
        copy.wait()
    count = jnp.zeros((tokens, atoms), F32)
    token_of = iota((tokens, atoms), 0) + r * tokens
    for j in range(cols):
        hit = (tok_all[j] == token_of).astype(F32)
        count = count + hit
        onehot[j] = hit.astype(BF16)
    count = 1.0 / jnp.sum(count, axis=1, keepdims=True)

    load_up.wait()
    for copy in atom_copies:
        copy.wait()
    total = jnp.zeros((tokens, width), F32)
    group = 4
    for j in range(0, cols, group):
        cells = atoms_all[pl.ds(j, group)].reshape(group * atoms, chans)
        up = jnp.maximum(dot(cells, v_up[...]), 0.0).astype(BF16)
        hits = jnp.concatenate([onehot[j + k] for k in range(group)], axis=1)
        total = total + dot(hits, up)
    act = total * count
    center = jnp.mean(act, axis=1, keepdims=True)
    spread = jnp.mean(act * act, axis=1, keepdims=True) - center * center
    normed = ((act - center) * lax.rsqrt(spread + EPS)).astype(BF16)
    projected = dot(normed, wsel[...])
    kv_own[...] = projected[:, 2 * LANES:].astype(BF16).reshape(kv_own.shape)
    kv_copies = [
        pltpu.make_async_remote_copy(
            src_ref=kv_own,
            dst_ref=kv_all.at[:, r],
            send_sem=kv_send.at[d],
            recv_sem=kv_recv.at[d],
            device_id=(lax.rem(r + d, rows), c),
            device_id_type=MESH,
        )
        for d in range(1, rows)
    ]
    for copy in kv_copies:
        copy.start()
    kv_all[:, r] = kv_own[...]
    head_q = projected[:, :LANES].astype(BF16)
    gate = jax.nn.sigmoid(projected[:, LANES:2 * LANES])
    act_t[...] = act.T
    load_o.wait()
    w_out_t[...] = v_o[...].T
    bias_in[c] = bias_out[c]

    for copy in kv_copies:
        copy.wait()
    for d in range(1, cols):
        col_copy(
            bias_out.at[lax.rem(c + d, cols)], bias_in.at[c], bias_send, bias_recv, d
        ).wait()
    key_vals = kv_all[...].reshape(cols * keys, LANES)
    scores = dot(head_q, key_vals, ((1,), (1,))) * head ** -0.5
    scores = scores + jnp.concatenate([bias_in[j].astype(F32) for j in range(cols)], axis=1)
    expo = jnp.exp(scores - jnp.max(scores, axis=1, keepdims=True))
    denom = jnp.sum(expo, axis=1, keepdims=True)
    gated = dot(expo.astype(BF16), key_vals) / denom * gate
    g_all[c] = gated.T[VOFF:VOFF + head].astype(BF16)
    g_copies = [col_copy(g_all.at[c], g_all.at[c], g_send, g_recv, d) for d in range(1, cols)]
    for copy in g_copies:
        copy.start()
    load_d.wait()
    w_down_t = v_d[...].T
    own_hits = onehot[c].astype(F32).T.astype(BF16)

    for copy in g_copies:
        copy.wait()
    mixed = dot(w_out_t[...], g_all[...].reshape(width, tokens))
    token_out = (act_t[...] + mixed).astype(BF16)
    token_down = dot(w_down_t, token_out).astype(BF16)
    final = atoms_all[c].astype(F32) + dot(own_hits, token_down, ((1,), (1,)))
    out_atom[...] = final.astype(BF16)
    w_out_t[:, 0:tokens] = token_out
    own = w_out_t[pl.ds(pl.multiple_of(c * head, head), head), 0:tokens]
    out_tok[...] = own.astype(F32).T.astype(BF16)


def body(
    atom_feat, atom_token, w_atom_qkv, w_atom_out, w_atom_up, pair_repr, w_bias, w_query, w_kv,
    w_gate, w_out, w_down,
):
    rows, cols = lax.axis_size("row"), lax.axis_size("col")
    atoms, chans = atom_feat.shape
    tokens, _, share, pair_width = pair_repr.shape
    keys = rows * share
    width = w_query.shape[0]
    head = width // cols
    heads = w_bias.shape[1]
    vmem = pltpu.VMEM
    sems = lambda n: pltpu.SemaphoreType.DMA((n,))
    return pl.pallas_call(
        kernel,
        out_shape=(
            jax.ShapeDtypeStruct((tokens, head), BF16),
            jax.ShapeDtypeStruct((atoms, chans), BF16),
        ),
        in_specs=[pl.BlockSpec(memory_space=pl.ANY)] * 12,
        out_specs=[pl.BlockSpec(memory_space=pltpu.VMEM)] * 2,
        scratch_shapes=[
            vmem(pair_repr.shape, BF16),
            vmem(w_atom_qkv.shape, BF16),
            vmem(w_atom_out.shape, BF16),
            vmem(w_atom_up.shape, BF16),
            vmem(w_bias.shape, F32),
            vmem((width, WINDOW), BF16),
            vmem((width, WINDOW), BF16),
            vmem((width, WINDOW), BF16),
            vmem((width, WINDOW), BF16),
            vmem(w_out.shape, BF16),
            vmem(w_down.shape, BF16),
            vmem((EXT, chans), BF16),
            vmem((cols, 1, atoms), jnp.int32),
            vmem((cols, atoms, chans), BF16),
            vmem((cols, tokens, atoms), BF16),
            vmem((heads * CHUNK, keys), F32),
            vmem((heads, tokens, keys), BF16),
            vmem((cols, tokens, keys), BF16),
            vmem((width, 3 * LANES), BF16),
            vmem(w_out.shape, BF16),
            vmem((width, tokens), F32),
            vmem((cols, share, LANES), BF16),
            vmem((cols, rows, share, LANES), BF16),
            vmem((cols, head, tokens), BF16),
            sems(13),
            sems(PIECES),
            sems(2),
            sems(2),
            sems(cols),
            sems(cols),
            sems(cols),
            sems(cols),
            sems(cols),
            sems(cols),
            sems(rows),
            sems(rows),
            sems(cols),
            sems(cols),
        ],
        compiler_params=pltpu.CompilerParams(
            collective_id=0, has_side_effects=True, vmem_limit_bytes=56 * 1024 * 1024
        ),
    )(
        atom_feat, atom_token.reshape(1, atoms), w_atom_qkv, w_atom_out, w_atom_up, pair_repr,
        w_bias, w_query, w_kv, w_gate, w_out, w_down,
    )


def solution(mesh):
    return jax.shard_map(
        body,
        mesh=mesh,
        in_specs=(
            P(("row", "col"), None),
            P(("row", "col")),
            P(),
            P(),
            P(),
            P("row", None, "col", None),
            P(),
            P(),
            P(),
            P(),
            P(),
            P(),
        ),
        out_specs=(P("row", "col"), P(("row", "col"), None)),
        check_vma=False,
    )
```

time: 455 us -> 49.9 us (0.11)
  waiting for transfers between devices: 267 us -> 0 us
  blocking collectives: 50.7 us -> 0 us
  matrix products: 46 us -> 0 us
  Pallas kernels: 0 us -> 44.2 us
  other arithmetic: 40.6 us -> 0 us
  local copies, waits for them, and re-layouts: 23 us -> 4.32 us
  between operations: 14.1 us -> 0.64 us
  starting transfers between devices: 11.8 us -> 0 us
    all_gather x2 -> x0, waiting for transfers between devices: 138 us -> none  [the longest x1 107 us: body(): bias_all = lax.all_gather(pair_bias, 'col', axis=2, tiled=True)]
    psum x2 -> x0, waiting for transfers between devices: 129 us -> none  [the longest x1 79 us: body(): token_down = lax.psum(down_part.astype(jnp.bfloat16), 'col')]
    dot_general x13 -> x0, matrix products: 46 us -> none  [the longest x1 17.7 us: body(): jnp.einsum('qhd,khd->hqk', query_heads, key_heads, preferred_element_type...]
    pallas_call x0 -> x1, Pallas kernels: none -> 44.2 us  [body(): pl.pallas_call(kernel, out_shape=(jax.ShapeDtypeStruct((tokens, head), BF...]
    psum x1 -> x0, blocking collectives: 34.5 us -> none  [body(): lax.psum(count_part.astype(jnp.bfloat16), 'col').astype(jnp.float32)]
    reduce_sum x5 -> x0, other arithmetic: 26.5 us -> none  [the longest x1 14.2 us: body(): denom = jnp.sum(expo, axis=-1)]
    all_gather x1 -> x0, blocking collectives: 16.2 us -> none  [body(): keyvals_rows = lax.all_gather(keyvals_local, 'row', axis=0, tiled=True)]
    slice x7 -> x0, local copies, waits for them, and re-layouts: 15.5 us -> none  [the longest x2 10.6 us: body(): keyvals_all[:, :model_width].reshape(key_count, head_count, head_size)]
  transfers between devices with their start and end apart: 6 -> 0, of which waited for: 4 -> 0; matrix products, arithmetic and copies ran while one was open for 10% -> 0% of each run, Pallas kernels for 0% -> 0%
where the time goes in v1:
time: 49.9 us; the launch traced here: 49.1 us
  Pallas kernels  44.2 us (89%)
  local copies, waits for them, and re-layouts  4.32 us (9%)
  between operations  0.64 us (1%)
    pallas_call x1, Pallas kernels, body(): pl.pallas_call(kernel, out_shape=(jax.ShapeDtypeStruct((tokens, head), BF...  44.2 us
    unnamed x2, local copies, waits for them, and re-layouts  2.79 us
    pallas_call x1, local copies, waits for them, and re-layouts, body(): pl.pallas_call(kernel, out_shape=(jax.ShapeDtypeStruct((tokens, head), BF...  1.53 us

profile of v1, /device:TPU:1, one launch (start us, length us, event | category | flops | bytes accessed | tf_op | source)
XLA Modules:
  0.0 49.1 jit_solution(5766793109988280352)
XLA Ops:
  0.6 1.4 %copy.14.w_bias = f32[128,16]{1,0:T(8,128)} copy(f32[128,16]{0,1:T(8,128)} %param.18) | data formatting | bytes 16384 | tf_op args[6]
  2.0 44.2 %shard_map.131 = (bf16[256,48]{1,0:T(8,128)(2,1)}, bf16[128,128]{1,0:T(8,128)(2,1)}) custom-call(bf16[128,128]{1,0:T(8,128)(2,1)} %feat.1, s32[1,128]{1,0:T(1,128)} %bitcast.1, bf16[128,384]{1,0:T(8,128)(2,1)} %w_qkv.1, bf16[128,128]{1,0:T(8,128)(2,1)} %w_ao.1, bf16[128,768]{1,0:T(8,128)(2,1)} %w_up.1, bf16[256,8,16,128]{3,2,1,0:T(8,128)(2,1)} %pair.1, ...), custom_call_target="tpu_custom_call" | custom-call | tf_op jit(solution)/shard_map/pallas_call | solution.py:335
  46.2 1.5 %copy.15 = bf16[256,48]{0,1:T(8,128)(2,1)} copy(bf16[256,48]{1,0:T(8,128)(2,1)} %get-tuple-element.2) | data formatting | bytes 49152 | tf_op jit(solution)/shard_map/pallas_call | solution.py:335
  47.8 1.4 %copy.17 = bf16[128,128]{1,0:T(8,128)(2,1)} copy(bf16[128,128]{1,0:T(8,128)(2,1)} %get-tuple-element.7) | data formatting | bytes 65536

commit v2 on v1

--- a/solution.py
+++ b/solution.py
@@ -18,9 +18,14 @@
 HALO = 48
 EXT = 256
 CHUNK = 16
-PIECES = 4
+PIECES = 8
+AHEAD = 2
+BEFORE = 1
+EARLY = 3
+EARLY_SENT = 3
 LANES = 128
 VOFF = 64
+ORDER = (5, 10, 15, 4, 1, 11, 14, 7, 8, 2, 13, 6, 9, 3, 12)
 WINDOW = 256
 
 
@@ -36,7 +41,7 @@
     feat, tok, w_qkv, w_ao, w_up, pair, w_bias, w_query, w_kv, w_gate, w_out, w_down,
     out_tok, out_atom,
     xbuf, v_qkv, v_ao, v_up, v_bias, v_q, v_k, v_v, v_g, v_o, v_d,
-    ext, tok_all, atoms_all, onehot, stage, bias_out, bias_in,
+    ext, tok_all, atoms_all, own_hits, total, count, stage, bias_out, bias_in,
     wsel, w_out_t, act_t, kv_own, kv_all, g_all,
     load_sem, pair_sem, halo_send, halo_recv, tok_send, tok_recv,
     atom_send, atom_recv, bias_send, bias_recv, kv_send, kv_recv, g_send, g_recv,
@@ -51,76 +56,41 @@
     width = w_query.shape[0]
     head = width // cols
 
-    loads = []
-
-    def load(src, dst, sem=None):
-        copy = pltpu.make_async_copy(src, dst, load_sem.at[len(loads)] if sem is None else sem)
-        copy.start()
-        if sem is None:
-            loads.append(copy)
-        return copy
-
-    load_feat = load(feat, ext.at[pl.ds(HALO, atoms)])
-    load_tok = load(tok, tok_all.at[c])
-    load_bias = load(w_bias, v_bias)
+    names = ("feat", "tok", "bias", "qkv", "ao", "up", "q", "g", "k", "v", "o", "d")
     part = tokens // PIECES
-    load_pair = [load(pair.at[pl.ds(0, part)], xbuf.at[pl.ds(0, part)], pair_sem.at[0])]
-    load_qkv = load(w_qkv, v_qkv)
-    load_ao = load(w_ao, v_ao)
-    for i in range(1, PIECES):
-        load_pair.append(
-            load(pair.at[pl.ds(i * part, part)], xbuf.at[pl.ds(i * part, part)], pair_sem.at[i])
-        )
-    load_up = load(w_up, v_up)
     first = jnp.minimum(c * head // LANES, (width - WINDOW) // LANES)
     begin = pl.multiple_of(first * LANES, LANES)
     window = pl.ds(begin, WINDOW)
-    load_q = load(w_query.at[:, window], v_q)
-    load_g = load(w_gate.at[:, window], v_g)
-    load_k = load(w_kv.at[:, window], v_k)
-    load_v = load(w_kv.at[:, pl.ds(pl.multiple_of(width + begin, LANES), WINDOW)], v_v)
-    load_o = load(w_out, v_o)
-    load_d = load(w_down, v_d)
-
-    barrier = pltpu.get_barrier_semaphore()
-    right, left = lax.rem(flat + 1, devices), lax.rem(flat + devices - 1, devices)
-
-    def coords(index):
-        return (index // cols, lax.rem(index, cols))
-
-    for peer in (left, right):
-        pl.semaphore_signal(barrier, inc=1, device_id=coords(peer), device_id_type=MESH)
-    for d in range(1, cols):
-        pl.semaphore_signal(
-            barrier, inc=1, device_id=(r, lax.rem(c + d, cols)), device_id_type=MESH
-        )
-    for d in range(1, rows):
-        pl.semaphore_signal(
-            barrier, inc=1, device_id=(lax.rem(r + d, rows), c), device_id_type=MESH
-        )
-    ext[pl.ds(atoms + 2 * HALO, EXT - atoms - 2 * HALO), :] = jnp.zeros(
-        (EXT - atoms - 2 * HALO, chans), BF16
-    )
-    pl.semaphore_wait(barrier, cols + rows)
-
-    to_right = pltpu.make_async_remote_copy(
-        src_ref=feat.at[pl.ds(atoms - HALO, HALO)],
-        dst_ref=ext.at[pl.ds(0, HALO)],
-        send_sem=halo_send.at[0],
-        recv_sem=halo_recv.at[0],
-        device_id=coords(right),
-        device_id_type=MESH,
-    )
-    to_left = pltpu.make_async_remote_copy(
-        src_ref=feat.at[pl.ds(0, HALO)],
-        dst_ref=ext.at[pl.ds(HALO + atoms, HALO)],
-        send_sem=halo_send.at[1],
-        recv_sem=halo_recv.at[1],
-        device_id=coords(left),
-        device_id_type=MESH,
-    )
-    to_right.start()
-    to_left.start()
+    beside = pl.ds(pl.multiple_of(width + begin, LANES), WINDOW)
+    ends = {
+        "feat": (feat, ext.at[pl.ds(HALO, atoms)]),
+        "tok": (tok, tok_all.at[c]),
+        "bias": (w_bias, v_bias),
+        "qkv": (w_qkv, v_qkv),
+        "ao": (w_ao, v_ao),
+        "up": (w_up, v_up),
+        "q": (w_query.at[:, window], v_q),
+        "g": (w_gate.at[:, window], v_g),
+        "k": (w_kv.at[:, window], v_k),
+        "v": (w_kv.at[:, beside], v_v),
+        "o": (w_out, v_o),
+        "d": (w_down, v_d),
+    }
+    loads = {
+        name: pltpu.make_async_copy(*ends[name], load_sem.at[i]) for i, name in enumerate(names)
+    }
+    pair_loads = [
+        pltpu.make_async_copy(
+            pair.at[pl.ds(i * part, part)], xbuf.at[pl.ds(i * part, part)], pair_sem.at[i]
+        )
+        for i in range(PIECES)
+    ]
+    for name in ("feat", "tok", "bias"):
+        loads[name].start()
+    for i in range(AHEAD):
+        pair_loads[i].start()
+    for name in ("qkv", "ao"):
+        loads[name].start()
 
     def col_copy(src, dst, send, recv, d):
         return pltpu.make_async_remote_copy(
@@ -132,16 +102,28 @@
             device_id_type=MESH,
         )
 
-    load_tok.wait()
-    tok_copies = [
-        col_copy(tok_all.at[c], tok_all.at[c], tok_send, tok_recv, d) for d in range(1, cols)
-    ]
-    for copy in tok_copies:
-        copy.start()
-
-    load_bias.wait()
-    eye = (iota((LANES, LANES), 0) == iota((LANES, LANES), 1)).astype(BF16)
-    wb_t = dot(v_bias[...].astype(BF16), eye, ((0,), (0,))).astype(BF16)
+    barrier = pltpu.get_barrier_semaphore()
+    right, left = lax.rem(flat + 1, devices), lax.rem(flat + devices - 1, devices)
+
+    def coords(index):
+        return (index // cols, lax.rem(index, cols))
+
+    for peer in (left, right):
+        pl.semaphore_signal(barrier, inc=1, device_id=coords(peer), device_id_type=MESH)
+    for d in range(1, cols):
+        pl.semaphore_signal(
+            barrier, inc=1, device_id=(r, lax.rem(c + d, cols)), device_id_type=MESH
+        )
+    for d in range(1, rows):
+        pl.semaphore_signal(
+            barrier, inc=1, device_id=(lax.rem(r + d, rows), c), device_id_type=MESH
+        )
+    ext[pl.ds(atoms + 2 * HALO, EXT - atoms - 2 * HALO), :] = jnp.zeros(
+        (EXT - atoms - 2 * HALO, chans), BF16
+    )
+
+    loads["bias"].wait()
+    wb_t = v_bias[...].astype(BF16)
     wb_sum = jnp.sum(wb_t.astype(F32), axis=1, keepdims=True)
     heads = wb_t.shape[0]
     lhs = jnp.concatenate([wb_t, jnp.ones((16, LANES), BF16)], axis=0)
@@ -174,7 +156,9 @@
         )
 
     def pair_piece(i):
-        load_pair[i].wait()
+        pair_loads[i].wait()
+        if i + AHEAD < PIECES:
+            pair_loads[i + AHEAD].start()
         steps = part // CHUNK
 
         def step(k, carry):
@@ -184,14 +168,49 @@
         lax.fori_loop(0, steps, step, 0)
 
     def send_piece(i):
-        for d in range(1, cols):
+        for d in ORDER:
             bias_copy(i, d).start()
 
-    pair_piece(0)
-
-    load_feat.wait()
-    load_qkv.wait()
-    load_ao.wait()
+    for i in range(BEFORE):
+        pair_piece(i)
+    pl.semaphore_wait(barrier, cols + rows)
+
+    to_right = pltpu.make_async_remote_copy(
+        src_ref=feat.at[pl.ds(atoms - HALO, HALO)],
+        dst_ref=ext.at[pl.ds(0, HALO)],
+        send_sem=halo_send.at[0],
+        recv_sem=halo_recv.at[0],
+        device_id=coords(right),
+        device_id_type=MESH,
+    )
+    to_left = pltpu.make_async_remote_copy(
+        src_ref=feat.at[pl.ds(0, HALO)],
+        dst_ref=ext.at[pl.ds(HALO + atoms, HALO)],
+        send_sem=halo_send.at[1],
+        recv_sem=halo_recv.at[1],
+        device_id=coords(left),
+        device_id_type=MESH,
+    )
+    to_right.start()
+    to_left.start()
+
+    loads["tok"].wait()
+    tok_copies = [
+        col_copy(tok_all.at[c], tok_all.at[c], tok_send, tok_recv, d) for d in range(1, cols)
+    ]
+    for copy in tok_copies:
+        copy.start()
+    for i in range(min(BEFORE, EARLY_SENT)):
+        send_piece(i)
+
+    for i in range(BEFORE, EARLY):
+        pair_piece(i)
+        if i < EARLY_SENT:
+            send_piece(i)
+
+    loads["feat"].wait()
+    loads["qkv"].wait()
+    loads["ao"].wait()
     to_right.wait()
     to_left.wait()
     proj = dot(ext[...], v_qkv[...]).astype(BF16)
@@ -218,49 +237,61 @@
     atom_out = ext[pl.ds(HALO, atoms), :].astype(F32) + dot(context.astype(BF16), v_ao[...])
     atoms_all[c] = atom_out.astype(BF16)
     atom_copies = [
-        col_copy(atoms_all.at[c], atoms_all.at[c], atom_send, atom_recv, d) for d in range(1, cols)
+        col_copy(atoms_all.at[c], atoms_all.at[c], atom_send, atom_recv, d) for d in ORDER
     ]
     for copy in atom_copies:
         copy.start()
 
-    send_piece(0)
-    for i in range(1, PIECES):
+    for name in ("up", "q", "g", "k", "v"):
+        loads[name].start()
+    for i in range(EARLY_SENT, EARLY):
+        send_piece(i)
+    for copy in tok_copies:
+        copy.wait()
+
+    token_of = iota((tokens, atoms), 0) + r * tokens
+    arrival = (0,) + ORDER
+    group = 4
+
+    def token_group(j):
+        cells, hits = [], []
+        for d in arrival[j * group:(j + 1) * group]:
+            if d:
+                atom_copies[ORDER.index(d)].wait()
+            slot = lax.rem(c + cols - d, cols)
+            cells.append(atoms_all[slot])
+            hits.append((tok_all[slot] == token_of).astype(F32))
+        if j == 0:
+            loads["up"].wait()
+            own_hits[...] = hits[0].T.astype(BF16)
+        up = jnp.maximum(dot(jnp.concatenate(cells, axis=0), v_up[...]), 0.0).astype(BF16)
+        added = dot(jnp.concatenate(hits, axis=1).astype(BF16), up)
+        counted = sum(hits[1:], hits[0])
+        total[...] = added if j == 0 else total[...] + added
+        count[...] = counted if j == 0 else count[...] + counted
+
+    for i in range(EARLY, PIECES):
         pair_piece(i)
         send_piece(i)
-
-    load_q.wait()
-    load_g.wait()
-    load_k.wait()
-    load_v.wait()
-    source = iota((WINDOW, LANES), 0) - (c * head - begin)
-    target = iota((WINDOW, LANES), 1)
-    pick_low = ((source == target) & (target < head)).astype(BF16)
-    pick_high = ((source == target - VOFF) & (target >= VOFF) & (target < VOFF + head)).astype(BF16)
-    wsel[:, 0:LANES] = dot(v_q[...], pick_low).astype(BF16)
-    wsel[:, LANES:2 * LANES] = dot(v_g[...], pick_high).astype(BF16)
-    wsel[:, 2 * LANES:] = (dot(v_k[...], pick_low) + dot(v_v[...], pick_high)).astype(BF16)
-
-    for copy in tok_copies:
-        copy.wait()
-    count = jnp.zeros((tokens, atoms), F32)
-    token_of = iota((tokens, atoms), 0) + r * tokens
-    for j in range(cols):
-        hit = (tok_all[j] == token_of).astype(F32)
-        count = count + hit
-        onehot[j] = hit.astype(BF16)
-    count = 1.0 / jnp.sum(count, axis=1, keepdims=True)
-
-    load_up.wait()
-    for copy in atom_copies:
-        copy.wait()
-    total = jnp.zeros((tokens, width), F32)
-    group = 4
-    for j in range(0, cols, group):
-        cells = atoms_all[pl.ds(j, group)].reshape(group * atoms, chans)
-        up = jnp.maximum(dot(cells, v_up[...]), 0.0).astype(BF16)
-        hits = jnp.concatenate([onehot[j + k] for k in range(group)], axis=1)
-        total = total + dot(hits, up)
-    act = total * count
+        if i == PIECES - 3:
+            loads["q"].wait()
+            loads["g"].wait()
+            loads["k"].wait()
+            loads["v"].wait()
+            source = iota((WINDOW, LANES), 0) - (c * head - begin)
+            target = iota((WINDOW, LANES), 1)
+            pick_low = ((source == target) & (target < head)).astype(BF16)
+            pick_high = ((source == target - VOFF) & (target >= VOFF) & (target < VOFF + head)).astype(BF16)
+            wsel[:, 0:LANES] = dot(v_q[...], pick_low).astype(BF16)
+            wsel[:, LANES:2 * LANES] = dot(v_g[...], pick_high).astype(BF16)
+            wsel[:, 2 * LANES:] = (dot(v_k[...], pick_low) + dot(v_v[...], pick_high)).astype(BF16)
+        if i >= PIECES - 2:
+            token_group(i - PIECES + 2)
+    for name in ("o", "d"):
+        loads[name].start()
+    for j in range(2, cols // group):
+        token_group(j)
+    act = total[...] * (1.0 / jnp.sum(count[...], axis=1, keepdims=True))
     center = jnp.mean(act, axis=1, keepdims=True)
     spread = jnp.mean(act * act, axis=1, keepdims=True) - center * center
     normed = ((act - center) * lax.rsqrt(spread + EPS)).astype(BF16)
@@ -283,7 +314,7 @@
     head_q = projected[:, :LANES].astype(BF16)
     gate = jax.nn.sigmoid(projected[:, LANES:2 * LANES])
     act_t[...] = act.T
-    load_o.wait()
+    loads["o"].wait()
     w_out_t[...] = v_o[...].T
     bias_in[c] = bias_out[c]
 
@@ -300,23 +331,26 @@
     denom = jnp.sum(expo, axis=1, keepdims=True)
     gated = dot(expo.astype(BF16), key_vals) / denom * gate
     g_all[c] = gated.T[VOFF:VOFF + head].astype(BF16)
-    g_copies = [col_copy(g_all.at[c], g_all.at[c], g_send, g_recv, d) for d in range(1, cols)]
+    g_copies = [col_copy(g_all.at[c], g_all.at[c], g_send, g_recv, d) for d in ORDER]
     for copy in g_copies:
         copy.start()
-    load_d.wait()
+    loads["d"].wait()
     w_down_t = v_d[...].T
-    own_hits = onehot[c].astype(F32).T.astype(BF16)
 
     for copy in g_copies:
         copy.wait()
     mixed = dot(w_out_t[...], g_all[...].reshape(width, tokens))
     token_out = (act_t[...] + mixed).astype(BF16)
     token_down = dot(w_down_t, token_out).astype(BF16)
-    final = atoms_all[c].astype(F32) + dot(own_hits, token_down, ((1,), (1,)))
+    final = atoms_all[c].astype(F32) + dot(own_hits[...], token_down, ((1,), (1,)))
     out_atom[...] = final.astype(BF16)
     w_out_t[:, 0:tokens] = token_out
-    own = w_out_t[pl.ds(pl.multiple_of(c * head, head), head), 0:tokens]
-    out_tok[...] = own.astype(F32).T.astype(BF16)
+    out_tok[...] = w_out_t[pl.ds(pl.multiple_of(c * head, head), head), 0:tokens]
+
+
+def hand_out(token_in, atom_in, token_out, atom_out):
+    token_out[...] = token_in[...]
+    atom_out[...] = atom_in[...]
 
 
 def body(
@@ -332,10 +366,10 @@
     heads = w_bias.shape[1]
     vmem = pltpu.VMEM
     sems = lambda n: pltpu.SemaphoreType.DMA((n,))
-    return pl.pallas_call(
+    token_out, atom_final = pl.pallas_call(
         kernel,
         out_shape=(
-            jax.ShapeDtypeStruct((tokens, head), BF16),
+            jax.ShapeDtypeStruct((head, tokens), BF16),
             jax.ShapeDtypeStruct((atoms, chans), BF16),
         ),
         in_specs=[pl.BlockSpec(memory_space=pl.ANY)] * 12,
@@ -345,7 +379,7 @@
             vmem(w_atom_qkv.shape, BF16),
             vmem(w_atom_out.shape, BF16),
             vmem(w_atom_up.shape, BF16),
-            vmem(w_bias.shape, F32),
+            vmem(w_bias.shape[::-1], F32),
             vmem((width, WINDOW), BF16),
             vmem((width, WINDOW), BF16),
             vmem((width, WINDOW), BF16),
@@ -355,7 +389,9 @@
             vmem((EXT, chans), BF16),
             vmem((cols, 1, atoms), jnp.int32),
             vmem((cols, atoms, chans), BF16),
-            vmem((cols, tokens, atoms), BF16),
+            vmem((atoms, tokens), BF16),
+            vmem((tokens, width), F32),
+            vmem((tokens, atoms), F32),
             vmem((heads * CHUNK, keys), F32),
             vmem((heads, tokens, keys), BF16),
             vmem((cols, tokens, keys), BF16),
@@ -385,8 +421,16 @@
         ),
     )(
         atom_feat, atom_token.reshape(1, atoms), w_atom_qkv, w_atom_out, w_atom_up, pair_repr,
-        w_bias, w_query, w_kv, w_gate, w_out, w_down,
-    )
+        w_bias.T, w_query, w_kv, w_gate, w_out, w_down,
+    )
+    token_out, atom_final = pl.pallas_call(
+        hand_out,
+        out_shape=(
+            jax.ShapeDtypeStruct((head, tokens), BF16),
+            jax.ShapeDtypeStruct((atoms, chans), BF16),
+        ),
+    )(token_out, atom_final)
+    return token_out.T, atom_final
 
 
 def solution(mesh):

time: 49.9 us -> 46.5 us (0.932); the launches traced: 49.1 us -> 46.3 us
  local copies, waits for them, and re-layouts: 4.32 us -> 0 us
  Pallas kernels: 44.2 us -> 45.7 us
    unnamed x2 -> x0, local copies, waits for them, and re-layouts: 2.79 us -> none
    pallas_call x1 -> x0, local copies, waits for them, and re-layouts: 1.53 us -> none  [body(): pl.pallas_call(kernel, out_shape=(jax.ShapeDtypeStruct((tokens, head), BF...]
    pallas_call x1 -> x2, Pallas kernels: 44.2 us -> 45.7 us  [the longest x1 44.3 us: body(): pl.pallas_call(kernel, out_shape=(jax.ShapeDtypeStruct((head, tokens), BF...]
where the time goes in v2:
time: 46.5 us; the launch traced here: 46.3 us
  Pallas kernels  45.7 us (98%)
  between operations  0.64 us (1%)
    pallas_call x1, Pallas kernels, body(): pl.pallas_call(kernel, out_shape=(jax.ShapeDtypeStruct((head, tokens), BF...  44.3 us
    pallas_call x1, Pallas kernels, body(): pl.pallas_call(hand_out, out_shape=(jax.ShapeDtypeStruct((head, tokens),...  1.4 us

profile of v2, /device:TPU:1, one launch (start us, length us, event | category | flops | bytes accessed | tf_op | source)
XLA Modules:
  0.0 46.3 jit_solution(5059137213282893013)
XLA Ops:
  0.6 44.3 %shard_map.131 = (bf16[48,256]{1,0:T(8,128)(2,1)}, bf16[128,128]{1,0:T(8,128)(2,1)}) custom-call(bf16[128,128]{1,0:T(8,128)(2,1)} %feat.1, s32[1,128]{1,0:T(1,128)} %bitcast.4, bf16[128,384]{1,0:T(8,128)(2,1)} %w_qkv.1, bf16[128,128]{1,0:T(8,128)(2,1)} %w_ao.1, bf16[128,768]{1,0:T(8,128)(2,1)} %w_up.1, bf16[256,8,16,128]{3,2,1,0:T(8,128)(2,1)} %pair.1, ...), custom_call_target="tpu_custom_call" | custom-call | tf_op jit(solution)/shard_map/pallas_call | solution.py:369
  44.9 1.4 %shard_map.132 = (bf16[48,256]{1,0:T(8,128)(2,1)}, bf16[128,128]{1,0:T(8,128)(2,1)}) custom-call(bf16[48,256]{1,0:T(8,128)(2,1)} %get-tuple-element.6.token_in, bf16[128,128]{1,0:T(8,128)(2,1)} %get-tuple-element.7.atom_in), custom_call_target="tpu_custom_call" | custom-call | tf_op jit(solution)/shard_map/pallas_call | solution.py:426

commit v3 on v2

--- a/solution.py
+++ b/solution.py
@@ -25,7 +25,9 @@
 EARLY_SENT = 3
 LANES = 128
 VOFF = 64
-ORDER = (5, 10, 15, 4, 1, 11, 14, 7, 8, 2, 13, 6, 9, 3, 12)
+HALVES = 2
+ORDER = (10, 9, 11, 8, 6, 5, 7, 4, 14, 13, 15, 12, 2, 1, 3)
+NEAR = (1, 3, 2)
 WINDOW = 256
 
 
@@ -42,7 +44,7 @@
     out_tok, out_atom,
     xbuf, v_qkv, v_ao, v_up, v_bias, v_q, v_k, v_v, v_g, v_o, v_d,
     ext, tok_all, atoms_all, own_hits, total, count, stage, bias_out, bias_in,
-    wsel, w_out_t, act_t, kv_own, kv_all, g_all,
+    wsel, w_out_t, act_t, tokens_t, kv_all, g_all,
     load_sem, pair_sem, halo_send, halo_recv, tok_send, tok_recv,
     atom_send, atom_recv, bias_send, bias_recv, kv_send, kv_recv, g_send, g_recv,
 ):
@@ -92,13 +94,22 @@
     for name in ("qkv", "ao"):
         loads[name].start()
 
+    side = 4
+    y, z = c // side, lax.rem(c, side)
+
+    def to(d):
+        return lax.rem(y + d % side, side) * side + lax.rem(z + d // side, side)
+
+    def source_of(d):
+        return lax.rem(y + side - d % side, side) * side + lax.rem(z + side - d // side, side)
+
     def col_copy(src, dst, send, recv, d):
         return pltpu.make_async_remote_copy(
             src_ref=src,
             dst_ref=dst,
             send_sem=send.at[d],
             recv_sem=recv.at[d],
-            device_id=(r, lax.rem(c + d, cols)),
+            device_id=(r, to(d)),
             device_id_type=MESH,
         )
 
@@ -152,7 +163,7 @@
     def bias_copy(i, d):
         span = pl.ds(i * part, part)
         return col_copy(
-            bias_out.at[lax.rem(c + d, cols), span], bias_in.at[c, span], bias_send, bias_recv, d
+            bias_out.at[to(d), span], bias_in.at[c, span], bias_send, bias_recv, d
         )
 
     def pair_piece(i):
@@ -258,7 +269,7 @@
         for d in arrival[j * group:(j + 1) * group]:
             if d:
                 atom_copies[ORDER.index(d)].wait()
-            slot = lax.rem(c + cols - d, cols)
+            slot = source_of(d)
             cells.append(atoms_all[slot])
             hits.append((tok_all[slot] == token_of).astype(F32))
         if j == 0:
@@ -280,11 +291,10 @@
             loads["v"].wait()
             source = iota((WINDOW, LANES), 0) - (c * head - begin)
             target = iota((WINDOW, LANES), 1)
-            pick_low = ((source == target) & (target < head)).astype(BF16)
-            pick_high = ((source == target - VOFF) & (target >= VOFF) & (target < VOFF + head)).astype(BF16)
-            wsel[:, 0:LANES] = dot(v_q[...], pick_low).astype(BF16)
-            wsel[:, LANES:2 * LANES] = dot(v_g[...], pick_high).astype(BF16)
-            wsel[:, 2 * LANES:] = (dot(v_k[...], pick_low) + dot(v_v[...], pick_high)).astype(BF16)
+            pick = (source == lax.rem(target, VOFF)) & (lax.rem(target, VOFF) < head)
+            pick = pick.astype(BF16)
+            for k, columns in enumerate((v_q, v_g, v_k, v_v)):
+                wsel[:, k * LANES:(k + 1) * LANES] = dot(columns[...], pick).astype(BF16)
         if i >= PIECES - 2:
             token_group(i - PIECES + 2)
     for name in ("o", "d"):
@@ -296,56 +306,109 @@
     spread = jnp.mean(act * act, axis=1, keepdims=True) - center * center
     normed = ((act - center) * lax.rsqrt(spread + EPS)).astype(BF16)
     projected = dot(normed, wsel[...])
-    kv_own[...] = projected[:, 2 * LANES:].astype(BF16).reshape(kv_own.shape)
-    kv_copies = [
-        pltpu.make_async_remote_copy(
-            src_ref=kv_own,
-            dst_ref=kv_all.at[:, r],
-            send_sem=kv_send.at[d],
-            recv_sem=kv_recv.at[d],
-            device_id=(lax.rem(r + d, rows), c),
+    half = tokens // 2
+    first_half = iota((half, LANES), 1) < VOFF
+    for k in (0, 1):
+        part_kv = projected[:, (2 + k) * LANES:(3 + k) * LANES]
+        packed = jnp.where(first_half, part_kv[:half], part_kv[half:]).astype(BF16)
+        kv_all[k, :, r] = packed.reshape(cols // 2, keys // rows, LANES)
+    cores = 2
+    x, core = r // cores, lax.rem(r, cores)
+    chips = rows // cores
+
+    def chip(dx):
+        return lax.rem(x + chips + dx, chips) * cores + core
+
+    def kv_hop(k, dx, over):
+        owner, target = (chip(-dx), x * cores + 1 - core) if over else (r, chip(dx))
+        return pltpu.make_async_remote_copy(
+            src_ref=kv_all.at[k, :, owner],
+            dst_ref=kv_all.at[k, :, owner],
+            send_sem=kv_send.at[k, dx, over],
+            recv_sem=kv_recv.at[k, dx, over],
+            device_id=(target, c),
             device_id_type=MESH,
         )
-        for d in range(1, rows)
-    ]
-    for copy in kv_copies:
-        copy.start()
-    kv_all[:, r] = kv_own[...]
-    head_q = projected[:, :LANES].astype(BF16)
-    gate = jax.nn.sigmoid(projected[:, LANES:2 * LANES])
+
+    for k in (0, 1):
+        for dx in NEAR:
+            kv_hop(k, dx, 0).start()
+        kv_hop(k, 0, 1).start()
+    low = iota((tokens, LANES), 1) < VOFF
+    both_q = projected[:, :LANES].astype(BF16)
+    q_low = jnp.where(low, both_q, jnp.zeros_like(both_q))
+    q_high = jnp.where(low, jnp.zeros_like(both_q), both_q)
+    gate_t = jax.nn.sigmoid(projected[:, LANES:2 * LANES]).T[:head]
     act_t[...] = act.T
     loads["o"].wait()
     w_out_t[...] = v_o[...].T
     bias_in[c] = bias_out[c]
 
-    for copy in kv_copies:
-        copy.wait()
+    for k in (0, 1):
+        for dx in NEAR:
+            kv_hop(k, dx, 0).wait()
+            kv_hop(k, dx, 1).start()
+    for dx in (0,) + NEAR:
+        kv_hop(0, dx, 1).wait()
     for d in range(1, cols):
         col_copy(
-            bias_out.at[lax.rem(c + d, cols)], bias_in.at[c], bias_send, bias_recv, d
+            bias_out.at[to(d)], bias_in.at[c], bias_send, bias_recv, d
         ).wait()
-    key_vals = kv_all[...].reshape(cols * keys, LANES)
-    scores = dot(head_q, key_vals, ((1,), (1,))) * head ** -0.5
-    scores = scores + jnp.concatenate([bias_in[j].astype(F32) for j in range(cols)], axis=1)
-    expo = jnp.exp(scores - jnp.max(scores, axis=1, keepdims=True))
-    denom = jnp.sum(expo, axis=1, keepdims=True)
-    gated = dot(expo.astype(BF16), key_vals) / denom * gate
-    g_all[c] = gated.T[VOFF:VOFF + head].astype(BF16)
-    g_copies = [col_copy(g_all.at[c], g_all.at[c], g_send, g_recv, d) for d in ORDER]
-    for copy in g_copies:
-        copy.start()
+    all_keys = kv_all[0].reshape(half * rows, LANES)
+    size = tokens // HALVES
+
+    def g_copy(t, d):
+        return pltpu.make_async_remote_copy(
+            src_ref=g_all.at[t, c],
+            dst_ref=g_all.at[t, c],
+            send_sem=g_send.at[t, d],
+            recv_sem=g_recv.at[t, d],
+            device_id=(r, to(d)),
+            device_id_type=MESH,
+        )
+
+    for t in range(HALVES):
+        span = slice(t * size, (t + 1) * size)
+        stacked = jnp.concatenate([q_low[span], q_high[span]], axis=0)
+        scores = dot(stacked, all_keys, ((1,), (1,))) * head ** -0.5
+        bias = jnp.concatenate(
+            [
+                jnp.concatenate([bias_in[j, span, :] for j in range(k, k + cols // 2)], axis=1)
+                for k in (0, cols // 2)
+            ],
+            axis=0,
+        )
+        scores = scores + bias.astype(F32)
+        top = jnp.max(jnp.maximum(scores[:size], scores[size:]), axis=1, keepdims=True)
+        expo = jnp.exp(scores - jnp.concatenate([top, top], axis=0))
+        denom = jnp.sum(expo[:size] + expo[size:], axis=1, keepdims=True)
+        if t == 0:
+            for dx in (0,) + NEAR:
+                kv_hop(1, dx, 1).wait()
+            all_values = kv_all[1].reshape(half * rows, LANES)
+        mixed = dot(expo.astype(BF16), all_values)
+        mixed = jnp.where(low[:size], mixed[:size], mixed[size:]) / denom
+        mixed = mixed.T
+        gated = (mixed[:head] + mixed[VOFF:VOFF + head]) * gate_t[:, span]
+        g_all[t, c] = gated.astype(BF16)
+        for d in ORDER:
+            g_copy(t, d).start()
     loads["d"].wait()
     w_down_t = v_d[...].T
-
-    for copy in g_copies:
-        copy.wait()
-    mixed = dot(w_out_t[...], g_all[...].reshape(width, tokens))
-    token_out = (act_t[...] + mixed).astype(BF16)
-    token_down = dot(w_down_t, token_out).astype(BF16)
-    final = atoms_all[c].astype(F32) + dot(own_hits[...], token_down, ((1,), (1,)))
+    own_atoms = atoms_all[c].astype(F32)
+
+    final = own_atoms
+    for t in range(HALVES):
+        span = slice(t * size, (t + 1) * size)
+        for d in ORDER:
+            g_copy(t, d).wait()
+        mixed = dot(w_out_t[...], g_all[t].reshape(width, size))
+        token_out = (act_t[:, span] + mixed).astype(BF16)
+        token_down = dot(w_down_t, token_out).astype(BF16)
+        final = final + dot(own_hits[:, span], token_down, ((1,), (1,)))
+        tokens_t[:, span] = token_out
     out_atom[...] = final.astype(BF16)
-    w_out_t[:, 0:tokens] = token_out
-    out_tok[...] = w_out_t[pl.ds(pl.multiple_of(c * head, head), head), 0:tokens]
+    out_tok[...] = tokens_t[pl.ds(pl.multiple_of(c * head, head), head), :]
 
 
 def hand_out(token_in, atom_in, token_out, atom_out):
@@ -365,7 +428,7 @@
     head = width // cols
     heads = w_bias.shape[1]
     vmem = pltpu.VMEM
-    sems = lambda n: pltpu.SemaphoreType.DMA((n,))
+    sems = pltpu.SemaphoreType.DMA
     token_out, atom_final = pl.pallas_call(
         kernel,
         out_shape=(
@@ -395,26 +458,26 @@
             vmem((heads * CHUNK, keys), F32),
             vmem((heads, tokens, keys), BF16),
             vmem((cols, tokens, keys), BF16),
-            vmem((width, 3 * LANES), BF16),
+            vmem((width, 4 * LANES), BF16),
             vmem(w_out.shape, BF16),
             vmem((width, tokens), F32),
-            vmem((cols, share, LANES), BF16),
-            vmem((cols, rows, share, LANES), BF16),
-            vmem((cols, head, tokens), BF16),
-            sems(13),
-            sems(PIECES),
-            sems(2),
-            sems(2),
-            sems(cols),
-            sems(cols),
-            sems(cols),
-            sems(cols),
-            sems(cols),
-            sems(cols),
-            sems(rows),
-            sems(rows),
-            sems(cols),
-            sems(cols),
+            vmem((width, tokens), BF16),
+            vmem((2, cols // 2, rows, share, LANES), BF16),
+            vmem((HALVES, cols, head, tokens // HALVES), BF16),
+            sems((13,)),
+            sems((PIECES,)),
+            sems((2,)),
+            sems((2,)),
+            sems((cols,)),
+            sems((cols,)),
+            sems((cols,)),
+            sems((cols,)),
+            sems((cols,)),
+            sems((cols,)),
+            sems((2, 4, 2)),
+            sems((2, 4, 2)),
+            sems((HALVES, cols)),
+            sems((HALVES, cols)),
         ],
         compiler_params=pltpu.CompilerParams(
             collective_id=0, has_side_effects=True, vmem_limit_bytes=56 * 1024 * 1024

time: 46.5 us -> 43.9 us (0.944)
  Pallas kernels: 45.7 us -> 43.1 us
    pallas_call x1, Pallas kernels: 44.3 us -> 41.7 us  [body(): pl.pallas_call(kernel, out_shape=(jax.ShapeDtypeStruct((head, tokens), BF...]
where the time goes in v3:
time: 43.9 us; the launch traced here: 43.7 us
  Pallas kernels  43.1 us (98%)
  between operations  0.64 us (1%)
    pallas_call x1, Pallas kernels, body(): pl.pallas_call(kernel, out_shape=(jax.ShapeDtypeStruct((head, tokens), BF...  41.7 us
    pallas_call x1, Pallas kernels, body(): pl.pallas_call(hand_out, out_shape=(jax.ShapeDtypeStruct((head, tokens),...  1.4 us

profile of v3, /device:TPU:1, one launch (start us, length us, event | category | flops | bytes accessed | tf_op | source)
XLA Modules:
  0.0 43.7 jit_solution(16936592657388096463)
XLA Ops:
  0.6 41.7 %shard_map.131 = (bf16[48,256]{1,0:T(8,128)(2,1)}, bf16[128,128]{1,0:T(8,128)(2,1)}) custom-call(bf16[128,128]{1,0:T(8,128)(2,1)} %feat.1, s32[1,128]{1,0:T(1,128)} %bitcast.4, bf16[128,384]{1,0:T(8,128)(2,1)} %w_qkv.1, bf16[128,128]{1,0:T(8,128)(2,1)} %w_ao.1, bf16[128,768]{1,0:T(8,128)(2,1)} %w_up.1, bf16[256,8,16,128]{3,2,1,0:T(8,128)(2,1)} %pair.1, ...), custom_call_target="tpu_custom_call" | custom-call | tf_op jit(solution)/shard_map/pallas_call | solution.py:432
  42.3 1.4 %shard_map.132 = (bf16[48,256]{1,0:T(8,128)(2,1)}, bf16[128,128]{1,0:T(8,128)(2,1)}) custom-call(bf16[48,256]{1,0:T(8,128)(2,1)} %get-tuple-element.6.token_in, bf16[128,128]{1,0:T(8,128)(2,1)} %get-tuple-element.7.atom_in), custom_call_target="tpu_custom_call" | custom-call | tf_op jit(solution)/shard_map/pallas_call | solution.py:489

commit v4 on v3

--- a/solution.py
+++ b/solution.py
@@ -19,6 +19,7 @@
 EXT = 256
 CHUNK = 16
 PIECES = 8
+TOGETHER = 2
 AHEAD = 2
 BEFORE = 1
 EARLY = 3
@@ -161,7 +162,7 @@
             bias_out[h, pl.ds(start, CHUNK), :] = stage[pl.ds(h * CHUNK, CHUNK), :].astype(BF16)
 
     def bias_copy(i, d):
-        span = pl.ds(i * part, part)
+        span = pl.ds((i + 1 - TOGETHER) * part, TOGETHER * part)
         return col_copy(
             bias_out.at[to(d), span], bias_in.at[c, span], bias_send, bias_recv, d
         )
@@ -179,6 +180,8 @@
         lax.fori_loop(0, steps, step, 0)
 
     def send_piece(i):
+        if (i + 1) % TOGETHER:
+            return
         for d in ORDER:
             bias_copy(i, d).start()
 

time: 43.9 us -> 43.2 us (0.984)
  Pallas kernels: 43.1 us -> 42.3 us
    pallas_call x1, Pallas kernels: 41.7 us -> 40.9 us  [body(): pl.pallas_call(kernel, out_shape=(jax.ShapeDtypeStruct((head, tokens), BF...]
where the time goes in v4:
time: 43.2 us; the launch traced here: 42.9 us
  Pallas kernels  42.3 us (98%)
  between operations  0.64 us (1%)
    pallas_call x1, Pallas kernels, body(): pl.pallas_call(kernel, out_shape=(jax.ShapeDtypeStruct((head, tokens), BF...  40.9 us
    pallas_call x1, Pallas kernels, body(): pl.pallas_call(hand_out, out_shape=(jax.ShapeDtypeStruct((head, tokens),...  1.4 us

profile of v4, /device:TPU:1, one launch (start us, length us, event | category | flops | bytes accessed | tf_op | source)
XLA Modules:
  0.0 42.9 jit_solution(16167328761518240198)
XLA Ops:
  0.6 40.9 %shard_map.131 = (bf16[48,256]{1,0:T(8,128)(2,1)}, bf16[128,128]{1,0:T(8,128)(2,1)}) custom-call(bf16[128,128]{1,0:T(8,128)(2,1)} %feat.1, s32[1,128]{1,0:T(1,128)} %bitcast.4, bf16[128,384]{1,0:T(8,128)(2,1)} %w_qkv.1, bf16[128,128]{1,0:T(8,128)(2,1)} %w_ao.1, bf16[128,768]{1,0:T(8,128)(2,1)} %w_up.1, bf16[256,8,16,128]{3,2,1,0:T(8,128)(2,1)} %pair.1, ...), custom_call_target="tpu_custom_call" | custom-call | tf_op jit(solution)/shard_map/pallas_call | solution.py:435
  41.5 1.4 %shard_map.132 = (bf16[48,256]{1,0:T(8,128)(2,1)}, bf16[128,128]{1,0:T(8,128)(2,1)}) custom-call(bf16[48,256]{1,0:T(8,128)(2,1)} %get-tuple-element.6.token_in, bf16[128,128]{1,0:T(8,128)(2,1)} %get-tuple-element.7.atom_in), custom_call_target="tpu_custom_call" | custom-call | tf_op jit(solution)/shard_map/pallas_call | solution.py:492

commit v5 on v4

--- a/solution.py
+++ b/solution.py
@@ -164,7 +164,11 @@
     def bias_copy(i, d):
         span = pl.ds((i + 1 - TOGETHER) * part, TOGETHER * part)
         return col_copy(
-            bias_out.at[to(d), span], bias_in.at[c, span], bias_send, bias_recv, d
+            bias_out.at[to(d), span],
+            bias_in.at[c, span],
+            bias_send.at[i * HALVES // PIECES],
+            bias_recv.at[i * HALVES // PIECES],
+            d,
         )
 
     def pair_piece(i):
@@ -286,7 +290,8 @@
 
     for i in range(EARLY, PIECES):
         pair_piece(i)
-        send_piece(i)
+        if i < PIECES - 1:
+            send_piece(i)
         if i == PIECES - 3:
             loads["q"].wait()
             loads["g"].wait()
@@ -337,6 +342,7 @@
         for dx in NEAR:
             kv_hop(k, dx, 0).start()
         kv_hop(k, 0, 1).start()
+    send_piece(PIECES - 1)
     low = iota((tokens, LANES), 1) < VOFF
     both_q = projected[:, :LANES].astype(BF16)
     q_low = jnp.where(low, both_q, jnp.zeros_like(both_q))
@@ -353,10 +359,6 @@
             kv_hop(k, dx, 1).start()
     for dx in (0,) + NEAR:
         kv_hop(0, dx, 1).wait()
-    for d in range(1, cols):
-        col_copy(
-            bias_out.at[to(d)], bias_in.at[c], bias_send, bias_recv, d
-        ).wait()
     all_keys = kv_all[0].reshape(half * rows, LANES)
     size = tokens // HALVES
 
@@ -372,6 +374,14 @@
 
     for t in range(HALVES):
         span = slice(t * size, (t + 1) * size)
+        for d in ORDER:
+            col_copy(
+                bias_out.at[to(d), pl.ds(t * size, size)],
+                bias_in.at[c, pl.ds(t * size, size)],
+                bias_send.at[t],
+                bias_recv.at[t],
+                d,
+            ).wait()
         stacked = jnp.concatenate([q_low[span], q_high[span]], axis=0)
         scores = dot(stacked, all_keys, ((1,), (1,))) * head ** -0.5
         bias = jnp.concatenate(
@@ -475,8 +485,8 @@
             sems((cols,)),
             sems((cols,)),
             sems((cols,)),
-            sems((cols,)),
-            sems((cols,)),
+            sems((HALVES, cols)),
+            sems((HALVES, cols)),
             sems((2, 4, 2)),
             sems((2, 4, 2)),
             sems((HALVES, cols)),

time: 43.2 us -> 43.7 us (1.012)
  Pallas kernels: 42.3 us -> 42.8 us
    pallas_call x1, Pallas kernels: 40.9 us -> 41.4 us  [body(): pl.pallas_call(kernel, out_shape=(jax.ShapeDtypeStruct((head, tokens), BF...]
where the time goes in v5:
time: 43.7 us; the launch traced here: 43.5 us
  Pallas kernels  42.8 us (98%)
  between operations  0.64 us (1%)
    pallas_call x1, Pallas kernels, body(): pl.pallas_call(kernel, out_shape=(jax.ShapeDtypeStruct((head, tokens), BF...  41.4 us
    pallas_call x1, Pallas kernels, body(): pl.pallas_call(hand_out, out_shape=(jax.ShapeDtypeStruct((head, tokens),...  1.4 us

profile of v5, /device:TPU:1, one launch (start us, length us, event | category | flops | bytes accessed | tf_op | source)
XLA Modules:
  0.0 43.5 jit_solution(151336898306453452)
XLA Ops:
  0.6 41.4 %shard_map.131 = (bf16[48,256]{1,0:T(8,128)(2,1)}, bf16[128,128]{1,0:T(8,128)(2,1)}) custom-call(bf16[128,128]{1,0:T(8,128)(2,1)} %feat.1, s32[1,128]{1,0:T(1,128)} %bitcast.4, bf16[128,384]{1,0:T(8,128)(2,1)} %w_qkv.1, bf16[128,128]{1,0:T(8,128)(2,1)} %w_ao.1, bf16[128,768]{1,0:T(8,128)(2,1)} %w_up.1, bf16[256,8,16,128]{3,2,1,0:T(8,128)(2,1)} %pair.1, ...), custom_call_target="tpu_custom_call" | custom-call | tf_op jit(solution)/shard_map/pallas_call | solution.py:445
  42.1 1.4 %shard_map.132 = (bf16[48,256]{1,0:T(8,128)(2,1)}, bf16[128,128]{1,0:T(8,128)(2,1)}) custom-call(bf16[48,256]{1,0:T(8,128)(2,1)} %get-tuple-element.6.token_in, bf16[128,128]{1,0:T(8,128)(2,1)} %get-tuple-element.7.atom_in), custom_call_target="tpu_custom_call" | custom-call | tf_op jit(solution)/shard_map/pallas_call | solution.py:502
